TPU v7x, 32 devices: a whole 2x2x4 slice. The times are simulated.
32 devices in a mesh: dp: 4 (over y, x), seq: 8 (over z, core).
Axes of the slice: x: 2, y: 2, z: 4, core: 2. Of those that a mesh axis runs over, the one named last changes fastest.
Arguments:
- tokens_in: bfloat16 [4, 1024, 768], P('dp', 'seq'), may hold values from -6 to 6
- cotangent: bfloat16 [4, 1024, 768], P('dp', 'seq'), may hold values from -6 to 6
- timesteps: int32 [4], P('dp'), may hold values from 0 to 999
- span_start: int32 [4], P('dp'), may hold values from 0 to 1023
- span_len: int32 [4], P('dp'), may hold values from 1 to 512
- vectors: float32 [9, 768], replicated, may hold values from -4 to 4, as said below
- w_ada: float32 [128, 4608], P(None, ('dp', 'seq')), may hold values from -0.5 to 0.5
- w_qkv: float32 [768, 2304], P(('dp', 'seq')), may hold values from -0.21875 to 0.21875
- w_attn: float32 [768, 768], P(('dp', 'seq')), may hold values from -3 to 3
- w_in: float32 [768, 3072], P(('dp', 'seq')), may hold values from -0.21875 to 0.21875
- w_out: float32 [3072, 768], P(('dp', 'seq')), may hold values from -0.109375 to 0.109375
- m_vec: float32 [9, 768], P(None, ('dp', 'seq')), may hold values from -0.0017089844 to 0.0017089844
- v_vec: float32 [9, 768], P(None, ('dp', 'seq')), may hold values from 1.1726959e-09 to 4.6907838e-09
- m_ada: float32 [128, 4608], P(None, ('dp', 'seq')), may hold values from -0.00061035156 to 0.00061035156
- v_ada: float32 [128, 4608], P(None, ('dp', 'seq')), may hold values from 1.3029955e-10 to 5.211982e-10
- m_qkv: float32 [768, 2304], P(('dp', 'seq')), may hold values from -0.00061035156 to 0.00061035156
- v_qkv: float32 [768, 2304], P(('dp', 'seq')), may hold values from 1.3029955e-10 to 5.211982e-10
- m_attn: float32 [768, 768], P(('dp', 'seq')), may hold values from -0.00061035156 to 0.00061035156
- v_attn: float32 [768, 768], P(('dp', 'seq')), may hold values from 1.3029955e-10 to 5.211982e-10
- m_in: float32 [768, 3072], P(('dp', 'seq')), may hold values from -0.00061035156 to 0.00061035156
- v_in: float32 [768, 3072], P(('dp', 'seq')), may hold values from 1.3029955e-10 to 5.211982e-10
- m_out: float32 [3072, 768], P(('dp', 'seq')), may hold values from -0.00061035156 to 0.00061035156
- v_out: float32 [3072, 768], P(('dp', 'seq')), may hold values from 1.3029955e-10 to 5.211982e-10
Outputs:
- block_out: bfloat16 [4, 1024, 768], P('dp', 'seq')
- grad_input: float32 [4, 1024, 768], P('dp', 'seq')
- grad_norm: float32 [], replicated
- vec_first: float32 [9, 768], P(None, ('dp', 'seq'))
- vec_second: float32 [9, 768], P(None, ('dp', 'seq'))
- vec_new: float32 [9, 768], P(None, ('dp', 'seq'))
- ada_first: float32 [128, 4608], P(None, ('dp', 'seq'))
- ada_second: float32 [128, 4608], P(None, ('dp', 'seq'))
- ada_new: float32 [128, 4608], P(None, ('dp', 'seq'))
- qkv_first: float32 [768, 2304], P(('dp', 'seq'))
- qkv_second: float32 [768, 2304], P(('dp', 'seq'))
- qkv_new: float32 [768, 2304], P(('dp', 'seq'))
- attn_first: float32 [768, 768], P(('dp', 'seq'))
- attn_second: float32 [768, 768], P(('dp', 'seq'))
- attn_new: float32 [768, 768], P(('dp', 'seq'))
- in_first: float32 [768, 3072], P(('dp', 'seq'))
- in_second: float32 [768, 3072], P(('dp', 'seq'))
- in_new: float32 [768, 3072], P(('dp', 'seq'))
- out_first: float32 [3072, 768], P(('dp', 'seq'))
- out_second: float32 [3072, 768], P(('dp', 'seq'))
- out_new: float32 [3072, 768], P(('dp', 'seq'))
Inputs may be any that keep to these rules, and one draw needn't show every extreme that they name: Rows 0 and 1 are the gains of the two norms, rows 2 to 7 the biases of the six modulation vectors in their order, row 8 the mask embedding.
All inputs are finite; a program needn't handle non-finite values.
Results may differ from a plain program's by a relative error of at most 0.02.
Values may be sent and summed in bfloat16 or wider, within the bound.
A program may use at most 192 MiB of HBM per device.

v0:
```python
from functools import partial
import math
from types import SimpleNamespace

import jax
import jax.numpy as jnp
from jax import lax
from jax.experimental import pallas as pl
from jax.experimental.pallas import tpu as pltpu
from jax.sharding import PartitionSpec as P

HD = 64
COND = 128
STEP = 10


BETA_ONE = 0.9
BETA_TWO = 0.999
ADAM_EPS = 1e-08
RATE = 0.1
RATE_VECTORS = 0.3
DECAY = 0.01
CLIP = 1.0
NORM_EPS = 1e-05


def cond_input(timesteps):
    half_cond = COND // 2
    freqs = jnp.exp(jnp.arange(half_cond, dtype=jnp.float32) * (-math.log(10000.0) / half_cond))
    angles = timesteps.astype(jnp.float32)[:, None] * freqs[None, :]
    return jax.nn.silu(jnp.concatenate([jnp.cos(angles), jnp.sin(angles)], axis=1))


def rotary_tables(positions):
    half_head = HD // 2
    inverse = jnp.exp(jnp.arange(half_head, dtype=jnp.float32) * (-math.log(10000.0) / half_head))
    angles = positions.astype(jnp.float32)[:, None] * inverse[None, :]
    return (jnp.cos(angles), jnp.sin(angles))


def rotate(values, cosines, sines):
    half_head = values.shape[-1] // 2
    first = values[..., :half_head]
    second = values[..., half_head:]
    cos_b = cosines[:, None, :]
    sin_b = sines[:, None, :]
    return jnp.concatenate(
        [first * cos_b - second * sin_b, second * cos_b + first * sin_b], axis=-1
    )


def rotate_back(grads, cosines, sines):
    half_head = grads.shape[-1] // 2
    first = grads[..., :half_head]
    second = grads[..., half_head:]
    cos_b = cosines[:, None, :]
    sin_b = sines[:, None, :]
    return jnp.concatenate(
        [first * cos_b + second * sin_b, second * cos_b - first * sin_b], axis=-1
    )


def normalize(values):
    centre = jnp.mean(values, axis=-1, keepdims=True)
    centred = values - centre
    inverse = lax.rsqrt(jnp.mean(centred * centred, axis=-1, keepdims=True) + NORM_EPS)
    return (centred * inverse, inverse)


def norm_back(normed, inverse, grad):
    return inverse * (
        grad
        - jnp.mean(grad, axis=-1, keepdims=True)
        - normed * jnp.mean(grad * normed, axis=-1, keepdims=True)
    )


def split_kv(block, width):
    seqs, block_rows = (block.shape[0], block.shape[1])
    keys = block[..., :width].reshape(seqs, block_rows, width // HD, HD)
    values = block[..., width:].reshape(seqs, block_rows, width // HD, HD)
    return (keys, values)


def attend_piece(carry, piece, queries, width, factor):
    piece_rows = piece.shape[1]
    size = math.gcd(piece_rows, 512)

    def attend_one_block(index, state):
        running, denom, accum = state
        block = lax.dynamic_slice_in_dim(piece, index * size, size, 1)
        keys, values = split_kv(block, width)
        scores = (
            jnp.einsum("sqhd,skhd->shqk", queries, keys, preferred_element_type=jnp.float32)
            * factor
        )
        highest = jnp.maximum(running, jnp.max(scores, axis=-1))
        shrink = jnp.exp(running - highest)
        weights = jnp.exp(scores - highest[..., None])
        denom = denom * shrink + jnp.sum(weights, axis=-1)
        accum = accum * shrink[..., None] + jnp.einsum(
            "shqk,skhd->shqd",
            weights.astype(jnp.bfloat16),
            values,
            preferred_element_type=jnp.float32,
        )
        return (highest, denom, accum)

    return lax.fori_loop(0, piece_rows // size, attend_one_block, carry)


def block_grads(block, queries, grad_out, logsum, delta, width, factor):
    keys, values = split_kv(block, width)
    scores = (
        jnp.einsum("sqhd,skhd->shqk", queries, keys, preferred_element_type=jnp.float32) * factor
    )
    probs = jnp.exp(scores - logsum[..., None])
    dprobs = jnp.einsum("sqhd,skhd->shqk", grad_out, values, preferred_element_type=jnp.float32)
    dscores = (probs * (dprobs - delta[..., None])).astype(jnp.bfloat16)
    return (keys, probs, dscores)


def query_grads(kv_all, queries, grad_out, logsum, delta, width, factor):
    total_rows = kv_all.shape[1]
    size = math.gcd(total_rows, 512)

    def query_one_block(index, accum):
        block = lax.dynamic_slice_in_dim(kv_all, index * size, size, 1)
        keys, probs, dscores = block_grads(block, queries, grad_out, logsum, delta, width, factor)
        return accum + factor * jnp.einsum(
            "shqk,skhd->sqhd", dscores, keys, preferred_element_type=jnp.float32
        )

    return lax.fori_loop(
        0, total_rows // size, query_one_block, jnp.zeros(queries.shape, jnp.float32)
    )


def key_grads(kv_all, queries, grad_out, logsum, delta, width, factor, count):
    size = math.gcd(count, 512)
    seqs = queries.shape[0]

    def key_one_block(index, accum):
        block = lax.dynamic_slice_in_dim(kv_all, index * size, size, 1)
        keys, probs, dscores = block_grads(block, queries, grad_out, logsum, delta, width, factor)
        grad_vals = jnp.einsum(
            "shqk,sqhd->skhd",
            probs.astype(jnp.bfloat16),
            grad_out,
            preferred_element_type=jnp.float32,
        )
        grad_keys = factor * jnp.einsum(
            "shqk,sqhd->skhd", dscores, queries, preferred_element_type=jnp.float32
        )
        joined = jnp.concatenate(
            [grad_keys.reshape(seqs, size, width), grad_vals.reshape(seqs, size, width)], axis=-1
        )
        return lax.dynamic_update_slice_in_dim(
            accum, jnp.transpose(joined, (1, 0, 2)), index * size, 0
        )

    initial = jnp.zeros((count, seqs, 2 * width), jnp.float32)
    return lax.fori_loop(0, count // size, key_one_block, initial)


def adam_step(weight, grad, first, second, rate, decay_rate):
    new_first = BETA_ONE * first + (1.0 - BETA_ONE) * grad
    new_second = BETA_TWO * second + (1.0 - BETA_TWO) * grad * grad
    fixed_first = new_first / (1.0 - BETA_ONE**STEP)
    fixed_second = new_second / (1.0 - BETA_TWO**STEP)
    new_weight = weight - rate * (
        fixed_first / (jnp.sqrt(fixed_second) + ADAM_EPS) + decay_rate * weight
    )
    return (new_first, new_second, new_weight)


def mod_back(grad_hidden, ln_values, normed, scale_part, gain):
    grad_shift = jnp.sum(grad_hidden, axis=1)
    grad_scale = jnp.sum(grad_hidden * ln_values, axis=1)
    grad_ln = grad_hidden * (1.0 + scale_part)
    grad_gain = jnp.sum(grad_ln * normed, axis=(0, 1))
    return (grad_shift, grad_scale, grad_gain, grad_ln * gain)


def plain(
    tokens_in,
    cotangent,
    timesteps,
    span_start,
    span_len,
    vectors,
    w_ada,
    w_qkv,
    w_attn,
    w_in,
    w_out,
    m_vec,
    v_vec,
    m_ada,
    v_ada,
    m_qkv,
    v_qkv,
    m_attn,
    v_attn,
    m_in,
    v_in,
    m_out,
    v_out,
):
    seqs, group, width = tokens_in.shape
    heads = width // HD
    factor = HD ** (-0.5)
    flat_rows = seqs * group
    full_ada, full_qkv, full_attn, full_in, full_out = (
        lax.all_gather(w_ada.astype(jnp.bfloat16), ("dp", "seq"), axis=1, tiled=True),
        lax.all_gather(w_qkv.astype(jnp.bfloat16), ("dp", "seq"), axis=0, tiled=True),
        lax.all_gather(w_attn.astype(jnp.bfloat16), ("dp", "seq"), axis=0, tiled=True),
        lax.all_gather(w_in.astype(jnp.bfloat16), ("dp", "seq"), axis=0, tiled=True),
        lax.all_gather(w_out.astype(jnp.bfloat16), ("dp", "seq"), axis=0, tiled=True),
    )
    positions = lax.axis_index("seq") * group + jnp.arange(group, dtype=jnp.int32)
    masked = (positions[None, :] >= span_start[:, None]) & (
        positions[None, :] < (span_start + span_len)[:, None]
    )
    cond_bf = cond_input(timesteps).astype(jnp.bfloat16)
    modulation = jnp.dot(cond_bf, full_ada, preferred_element_type=jnp.float32) + vectors[
        2:8
    ].reshape(1, 6 * width)
    pieces = [modulation[:, which * width : (which + 1) * width][:, None, :] for which in range(6)]
    shift_one, scale_one, gate_one, shift_two, scale_two, gate_two = pieces
    start_tokens = jnp.where(
        masked[..., None], vectors[8][None, None, :], tokens_in.astype(jnp.float32)
    )
    normed_one, inv_one = normalize(start_tokens)
    ln_one = normed_one * vectors[0]
    hidden_one = (
        (ln_one * (1.0 + scale_one) + shift_one).astype(jnp.bfloat16).reshape(flat_rows, width)
    )
    projected = jnp.dot(hidden_one, full_qkv, preferred_element_type=jnp.float32).reshape(
        seqs, group, 3 * width
    )
    cosines, sines = rotary_tables(positions)
    queries = rotate(projected[..., :width].reshape(seqs, group, heads, HD), cosines, sines).astype(
        jnp.bfloat16
    )
    keys_here = rotate(
        projected[..., width : 2 * width].reshape(seqs, group, heads, HD), cosines, sines
    ).astype(jnp.bfloat16)
    values_here = projected[..., 2 * width :].astype(jnp.bfloat16)
    kv_local = jnp.concatenate([keys_here.reshape(seqs, group, width), values_here], axis=-1)
    initial = (
        jnp.full((seqs, heads, group), -1e30, jnp.float32),
        jnp.zeros((seqs, heads, group), jnp.float32),
        jnp.zeros((seqs, heads, group, HD), jnp.float32),
    )
    running, denom, accum = attend_piece(
        initial, lax.all_gather(kv_local, "seq", axis=1, tiled=True), queries, width, factor
    )
    attn_heads = accum / denom[..., None]
    logsum = running + jnp.log(denom)
    attn_rows = jnp.transpose(attn_heads, (0, 2, 1, 3)).reshape(flat_rows, width)
    attn_bf = attn_rows.astype(jnp.bfloat16)
    branch_one = jnp.dot(attn_bf, full_attn, preferred_element_type=jnp.float32).reshape(
        seqs, group, width
    )
    mid_tokens = start_tokens + gate_one * branch_one
    normed_two, inv_two = normalize(mid_tokens)
    ln_two = normed_two * vectors[1]
    hidden_two = (
        (ln_two * (1.0 + scale_two) + shift_two).astype(jnp.bfloat16).reshape(flat_rows, width)
    )
    pre_act = jnp.dot(hidden_two, full_in, preferred_element_type=jnp.float32)
    activ, gelu_back = jax.vjp(partial(jax.nn.gelu, approximate=True), pre_act)
    activ_bf = activ.astype(jnp.bfloat16)
    branch_two = jnp.dot(activ_bf, full_out, preferred_element_type=jnp.float32).reshape(
        seqs, group, width
    )
    block_out = (mid_tokens + gate_two * branch_two).astype(jnp.bfloat16)
    grad_y = cotangent.astype(jnp.float32)
    grad_gate_two = jnp.sum(grad_y * branch_two, axis=1)
    grad_branch_two = (grad_y * gate_two).astype(jnp.bfloat16).reshape(flat_rows, width)
    grad_w_out = jnp.dot(activ_bf.T, grad_branch_two, preferred_element_type=jnp.float32)
    grad_activ = jnp.dot(grad_branch_two, full_out.T, preferred_element_type=jnp.float32)
    grad_pre = gelu_back(grad_activ)[0].astype(jnp.bfloat16)
    grad_w_in = jnp.dot(hidden_two.T, grad_pre, preferred_element_type=jnp.float32)
    grad_hidden_two = jnp.dot(grad_pre, full_in.T, preferred_element_type=jnp.float32).reshape(
        seqs, group, width
    )
    grad_shift_two, grad_scale_two, grad_gain_two, grad_normed_two = mod_back(
        grad_hidden_two, ln_two, normed_two, scale_two, vectors[1]
    )
    grad_mid = grad_y + norm_back(normed_two, inv_two, grad_normed_two)
    grad_gate_one = jnp.sum(grad_mid * branch_one, axis=1)
    grad_branch_one = (grad_mid * gate_one).astype(jnp.bfloat16).reshape(flat_rows, width)
    grad_w_attn = jnp.dot(attn_bf.T, grad_branch_one, preferred_element_type=jnp.float32)
    grad_attn_bf = (
        jnp.dot(grad_branch_one, full_attn.T, preferred_element_type=jnp.float32)
        .astype(jnp.bfloat16)
        .reshape(seqs, group, heads, HD)
    )
    delta = jnp.einsum("sqhd,shqd->shq", grad_attn_bf.astype(jnp.float32), attn_heads)
    kv_all = lax.all_gather(kv_local, "seq", axis=1, tiled=True)
    grad_queries = query_grads(kv_all, queries, grad_attn_bf, logsum, delta, width, factor)
    grad_kv = jnp.transpose(
        lax.psum_scatter(
            key_grads(
                kv_all,
                queries,
                grad_attn_bf,
                logsum,
                delta,
                width,
                factor,
                group * lax.axis_size("seq"),
            ).astype(jnp.bfloat16),
            "seq",
            scatter_dimension=0,
            tiled=True,
        ).astype(jnp.float32),
        (1, 0, 2),
    )
    grad_keys = grad_kv[..., :width].reshape(seqs, group, heads, HD)
    grad_qkv = jnp.concatenate(
        [
            rotate_back(grad_queries, cosines, sines).reshape(seqs, group, width),
            rotate_back(grad_keys, cosines, sines).reshape(seqs, group, width),
            grad_kv[..., width:],
        ],
        axis=-1,
    )
    grad_qkv = grad_qkv.astype(jnp.bfloat16).reshape(flat_rows, 3 * width)
    grad_w_qkv = jnp.dot(hidden_one.T, grad_qkv, preferred_element_type=jnp.float32)
    grad_hidden_one = jnp.dot(grad_qkv, full_qkv.T, preferred_element_type=jnp.float32).reshape(
        seqs, group, width
    )
    grad_shift_one, grad_scale_one, grad_gain_one, grad_normed_one = mod_back(
        grad_hidden_one, ln_one, normed_one, scale_one, vectors[0]
    )
    grad_start = grad_mid + norm_back(normed_one, inv_one, grad_normed_one)
    grad_mask_row = jnp.sum(jnp.where(masked[..., None], grad_start, 0.0), axis=(0, 1))
    grad_input = jnp.where(masked[..., None], 0.0, grad_start)
    grad_mod = jnp.concatenate(
        [
            grad_shift_one,
            grad_scale_one,
            grad_gate_one,
            grad_shift_two,
            grad_scale_two,
            grad_gate_two,
        ],
        axis=1,
    )
    grad_w_ada = jnp.dot(cond_bf.astype(jnp.float32).T, grad_mod, precision=lax.Precision.HIGHEST)
    grad_vectors = jnp.concatenate(
        [
            grad_gain_one[None, :],
            grad_gain_two[None, :],
            jnp.sum(grad_mod, axis=0).reshape(6, width),
            grad_mask_row[None, :],
        ],
        axis=0,
    )
    red_ada, red_qkv, red_attn, red_in, red_out, red_vec = (
        lax.psum_scatter(grad_w_ada, ("dp", "seq"), scatter_dimension=1, tiled=True),
        lax.psum_scatter(grad_w_qkv, ("dp", "seq"), scatter_dimension=0, tiled=True),
        lax.psum_scatter(grad_w_attn, ("dp", "seq"), scatter_dimension=0, tiled=True),
        lax.psum_scatter(grad_w_in, ("dp", "seq"), scatter_dimension=0, tiled=True),
        lax.psum_scatter(grad_w_out, ("dp", "seq"), scatter_dimension=0, tiled=True),
        lax.psum_scatter(grad_vectors, ("dp", "seq"), scatter_dimension=1, tiled=True),
    )
    local_squares = jnp.float32(0.0)
    for reduced in (red_vec, red_ada, red_qkv, red_attn, red_in, red_out):
        local_squares = local_squares + jnp.sum(reduced * reduced)
    grad_norm = jnp.sqrt(lax.psum(local_squares, ("dp", "seq")))
    clip_factor = jnp.minimum(1.0, CLIP / (grad_norm + 1e-06))
    columns = red_vec.shape[1]
    own_vectors = lax.dynamic_slice_in_dim(
        vectors, lax.axis_index(("dp", "seq")) * columns, columns, 1
    )
    vec_out = adam_step(own_vectors, red_vec * clip_factor, m_vec, v_vec, RATE_VECTORS, 0.0)
    ada_out = adam_step(w_ada, red_ada * clip_factor, m_ada, v_ada, RATE, DECAY)
    qkv_out = adam_step(w_qkv, red_qkv * clip_factor, m_qkv, v_qkv, RATE, DECAY)
    attn_out = adam_step(w_attn, red_attn * clip_factor, m_attn, v_attn, RATE, DECAY)
    in_out = adam_step(w_in, red_in * clip_factor, m_in, v_in, RATE, DECAY)
    out_out = adam_step(w_out, red_out * clip_factor, m_out, v_out, RATE, DECAY)
    return (
        block_out,
        grad_input,
        grad_norm,
        vec_out[0],
        vec_out[1],
        vec_out[2],
        ada_out[0],
        ada_out[1],
        ada_out[2],
        qkv_out[0],
        qkv_out[1],
        qkv_out[2],
        attn_out[0],
        attn_out[1],
        attn_out[2],
        in_out[0],
        in_out[1],
        in_out[2],
        out_out[0],
        out_out[1],
        out_out[2],
    )


F32, BF = jnp.float32, jnp.bfloat16
MESH = pl.DeviceIdType.MESH
DP, LINE, SEQ, CHIPS, ALL = 4, 4, 8, 16, 32
ROWS, WIDTH, PACK = 128, 768, 640
HALF = WIDTH // 2
HALVES = ((0, 0), (0, 1), (0, 2), (2, 2), (1, 0), (1, 1), (1, 2), None, (2, 0), (2, 1))

def numbered(**counts):
    at = {}
    for name, count in counts.items():
        at[name] = sum(counts[other] for other in at)
    return SimpleNamespace(**at), sum(counts.values())


S, SEM_COUNT = numbered(
    load=11,
    cond=1,
    mix_qkv=1,
    mix_in=1,
    mix_attn=1,
    mod=1,
    w_qkv=1,
    w_attn=4,
    plane_in=1,
    w_in=4,
    w_out=4,
    group_qkv=4,
    group_attn=4,
    fw_qkv=1,
    fw_attn=1,
    fw_in=1,
    fw_out=1,
    tok=4,
    h2=4,
    dm=4,
    xf=4,
    o=1,
    mm=1,
    dh2=1,
    do=1,
    gp=1,
    dh1=5,
    pair_out=1,
    pair_in=1,
    pair_attn=1,
    pair_qkv=1,
    plane_attn=1,
    plane_qkv=1,
    line_out=5,
    line_in=5,
    slice_in=1,
    line_attn=1,
    line_qkv=1,
    last_in=1,
    last_attn=1,
    last_qkv=1,
    early=7,
    late=7,
    sq=1,
)

SCRATCH = dict(
    i_tok=((1, 128, 768), BF),
    i_cot=((1, 128, 768), BF),
    i_vec=((9, 768), F32),
    i_wada=((144, 128), F32),
    i_wqkv=((24, 2304), F32),
    i_wattn=((24, 768), F32),
    i_win=((24, 3072), F32),
    i_wout=((96, 768), F32),
    wide_qkv=((48, 3072), F32),
    wide_in=((48, 3072), F32),
    wide_attn=((48, 768), F32),
    s_qkv=((48, 3072), BF),
    s_in=((48, 3072), BF),
    s_attn=((48, 768), BF),
    w_qkv=((768, 768), BF),
    w_in=((4, 4, 48, 768), BF),
    w_attn=((768, 768), BF),
    w_out=((4, 2, 96, 768), BF),
    t_w_qkv=((640, 768), BF),
    t_w_attn=((768, 1024), BF),
    t_w_in=((768, 768), BF),
    t_w_out=((768, 768), BF),
    t_h1=((768, 512), BF),
    conds_all=((4, 8, 128), F32),
    mod_send=((4, 4, 128), F32),
    mod_got=((32, 4, 128), F32),
    mod_flat=((40, 128), F32),
    mod_pad=((8, 384), F32),
    turn=((2, 4, 128, 128), F32),
    dmod_flat=((4, 40, 128), F32),
    mod=((8, 768), F32),
    x0=((128, 768), F32),
    n1=((4, 128, 768), F32),
    inv1=((4, 128, 128), F32),
    x1=((128, 768), F32),
    n2=((128, 768), F32),
    inv2=((128, 128), F32),
    a=((128, 768), F32),
    dx1=((128, 768), F32),
    toks=((4, 128, 768), BF),
    h1=((4, 128, 768), BF),
    h2=((4, 128, 768), BF),
    dm=((4, 128, 768), BF),
    gb=((4, 128, 768), BF),
    du=((4, 128, 768), BF),
    xb=((2, 4, 128, 640), BF),
    pt=((3, 1024, 512), BF),
    vt=((2, 128, 1024), BF),
    kt=((2, 128, 1024), BF),
    back=((4, 128, 768), F32),
    ot=((2, 128, 512), F32),
    os=((4, 192, 128), BF),
    ob=((4, 192, 128), BF),
    o2=((4, 128, 128), BF),
    mms=((4, 128, 768), BF),
    mmr=((4, 128, 768), BF),
    dhs=((4, 128, 768), BF),
    dhr=((4, 128, 768), BF),
    das=((128, 768), BF),
    dos=((4, 192, 128), BF),
    dob=((4, 192, 128), BF),
    dst=((3, 1024, 512), BF),
    ga=((512, 640), F32),
    gps=((512, 512), BF),
    gpr=((512, 512), BF),
    dqkv=((4, 128, 768), BF),
    d1s=((4, 128, 768), BF),
    d1r=((4, 128, 768), BF),
    g_out=((4, 2, 96, 768), BF),
    g_in=((2, 4, 4, 48, 384), BF),
    g_attn=((2, 768, 384), BF),
    g_qkv=((2, 768, 384), BF),
    p_out=((4, 96, 768), BF),
    p_in=((4, 4, 48, 384), BF),
    p_attn=((768, 384), BF),
    p_qkv=((768, 384), BF),
    q_attn=((4, 192, 384), BF),
    q_qkv=((4, 192, 384), BF),
    m_attn=((192, 384), BF),
    m_qkv=((192, 384), BF),
    r_out=((4, 96, 768), BF),
    r_in=((4, 4, 48, 384), BF),
    via_in=((4, 48, 384), BF),
    via_out=((96, 768), BF),
    via_dh1=((128, 768), BF),
    m_in=((4, 48, 384), BF),
    u_in=((4, 48, 384), BF),
    r_attn=((4, 48, 384), BF),
    r_qkv=((4, 48, 384), BF),
    t_in=((4, 48, 384), F32),
    t_attn=((1, 48, 384), F32),
    t_qkv=((4, 48, 384), F32),
    f_in=((4, 2, 24, 384), F32),
    f_attn=((1, 2, 24, 384), F32),
    f_qkv=((4, 2, 24, 384), F32),
    early=((8, 768), F32),
    early_pair=((8, 768), F32),
    early_line=((4, 8, 384), F32),
    early_plane=((4, 8, 384), F32),
    early_all=((2, 4, 8, 384), F32),
    late=((4, 768), F32),
    late_pair=((4, 768), F32),
    late_line=((4, 4, 384), F32),
    late_plane=((4, 4, 384), F32),
    late_all=((2, 4, 4, 384), F32),
    sq=((32, 1, 128), F32),
)


def dot(left, right):
    return jnp.dot(left, right, preferred_element_type=F32)


def dot_nt(left, right):
    return lax.dot_general(left, right, (((1,), (1,)), ((), ())), preferred_element_type=F32)


def dot_tn(left, right):
    return lax.dot_general(left, right, (((0,), (0,)), ((), ())), preferred_element_type=F32)


def loop(count, body, start=0):
    def step(index, carry):
        body(index)
        return carry

    lax.fori_loop(start, count, step, 0)


def layer_kernel(
    i_time,
    i_start,
    i_len,
    h_tok,
    h_cot,
    h_vec,
    h_wada,
    h_wqkv,
    h_wattn,
    h_win,
    h_wout,
    o_y,
    o_dx,
    o_norm,
    o_gqkv,
    o_gattn,
    o_gin,
    o_gout,
    o_dmod,
    o_gvec,
    o_vec,
    o_conds,
    *scratch,
):
    r = SimpleNamespace(**dict(zip(SCRATCH, scratch)), when=scratch[-3])
    send_sems, recv_sems = scratch[-2:]
    i_tok, i_cot, i_vec, i_wada = r.i_tok, r.i_cot, r.i_vec, r.i_wada
    i_wqkv, i_wattn, i_win, i_wout = r.i_wqkv, r.i_wattn, r.i_win, r.i_wout
    b, s = lax.axis_index("dp"), lax.axis_index("seq")
    z, c = lax.div(s, 2), lax.rem(s, 2)
    mate = s + 1 - 2 * c
    chip = b * LINE + z
    me = b * SEQ + s
    drains = []

    def push(src, dst, at, to_b, to_s, out=None):
        pltpu.make_async_remote_copy(
            src_ref=src,
            dst_ref=dst,
            send_sem=send_sems.at[at if out is None else out],
            recv_sem=recv_sems.at[at],
            device_id=(to_b, to_s),
            device_id_type=MESH,
        ).start()

    def keep(src, dst, at):
        pltpu.make_async_copy(src, dst, recv_sems.at[at]).start()

    def got(at, like):
        pltpu.make_async_copy(like, like, recv_sems.at[at]).wait()

    def left(at, like):
        pltpu.make_async_copy(like, like, send_sems.at[at]).wait()

    def sent(at, like):
        drains.append(lambda: left(at, like))

    def by_core(body):
        for h, width in ((0, HALF), (1, PACK - HALF)):

            @pl.when(c == h)
            def _():
                body(slice(HALF * h, HALF * h + width), width)

    def sent_by_core(at, like):
        drains.append(lambda: by_core(lambda columns, width: left(at, like(width))))

    near = (b, b + 1 - 2 * lax.rem(b, 2), b + 2 - 4 * lax.div(b, 2), 3 - b)

    def toward(k):
        if k == 3:
            return 3, near[3]
        slot = 1 + c if k == 1 else 2 - c
        return slot, (1 - c) * near[k] + c * near[3 - k]

    def peers(body):
        for k in (1, 2, 3):
            body(*toward(k))

    def stack(body):
        for k in (1, 2, 3):
            body(lax.rem(z + k + 2 * c * (2 - k), LINE))

    def line_gather(block, at, near=True, rest=True):
        inner = 1 + lax.rem(z, 2)
        if near:
            push(block(z), block(z), at + z, b, 2 * inner + c, at)

        def one(to):
            relayed = ((z == 1) & (to == 3)) | ((z == 2) & (to == 0))

            @pl.when(jnp.logical_not(relayed | (to == inner)))
            def _():
                push(block(z), block(z), at + z, b, 2 * to + c, at)

        if rest:
            stack(one)

    def line_relay(block, at):
        for middle, source, to in ((2, 1, 3), (1, 2, 0)):

            @pl.when(z == middle)
            def _():
                got(at + source, block(source))
                push(block(source), block(source), at + source, b, 2 * to + c, at)

    def line_got(block, at, k):
        here = (k == z) | ((z == 2) & (k == 1)) | ((z == 1) & (k == 2))

        @pl.when(jnp.logical_not(here))
        def _():
            got(at + k, block(0))

    far = lax.div(z, 2)

    def line_order(j):
        return lax.rem(z + (2, 3 - 2 * far, 1 + 2 * far, 0)[j], LINE)

    def line_add(j, rows, dst, via, at):
        to = line_order(j)
        outer_chip = (z == 0) | (z == 3)

        def direct():
            push(rows(to), dst.at[z], at + z, b, 2 * to + c, at)

        if j == 0:

            @pl.when(outer_chip)
            def _():
                push(rows(to), via, at + 4, b, 2 * (1 + far) + c, at)

            @pl.when(jnp.logical_not(outer_chip))
            def _():
                direct()

        elif j < 3:
            direct()
        else:
            keep(rows(z), dst.at[z], at + z)

    def line_via(via, at, add):
        @pl.when((z == 1) | (z == 2))
        def _():
            got(at + 4, via)
            add()

    def line_done(dst, at):
        for k in range(4):
            missing = ((z == 1) & (k == 3)) | ((z == 2) & (k == 0))

            @pl.when(jnp.logical_not(missing))
            def _():
                got(at + k, dst.at[k])

    def line_clear(dst):
        for middle, k in ((1, 3), (2, 0)):

            @pl.when(z == middle)
            def _():
                dst[k] = jnp.zeros(dst.shape[1:], BF)

    lane = lax.broadcasted_iota(jnp.int32, (1, 128), 1)
    low = lane < 64
    own24 = pl.ds(pl.multiple_of(24 * c, 8), 24)
    mate24 = pl.ds(pl.multiple_of(24 * (1 - c), 8), 24)
    part = pl.ds(pl.multiple_of(HALF * c, 128), HALF)
    chip_rows = pl.ds(pl.multiple_of(48 * chip, 16), 48)
    group_rows = pl.ds(pl.multiple_of(192 * b, 16), 192)

    barrier = pltpu.get_barrier_semaphore()

    def greet(k):
        other = lax.rem(me + k, ALL)
        pl.semaphore_signal(
            barrier, inc=1, device_id=(lax.div(other, SEQ), lax.rem(other, SEQ)), device_id_type=MESH
        )

    loads = (
        (i_time, r.when.at[0]),
        (i_start, r.when.at[1]),
        (i_len, r.when.at[2]),
        (h_wqkv, i_wqkv),
        (h_win, i_win),
        (h_wattn, i_wattn),
        (h_wout, i_wout),
        (h_tok, i_tok),
        (h_vec, i_vec),
        (h_wada, i_wada),
        (h_cot, i_cot),
    )
    for k, (src, dst) in enumerate(loads):
        pltpu.make_async_copy(src, dst, recv_sems.at[S.load + k]).start()
    loop(ALL, greet, 1)
    for k, (src, dst) in enumerate(loads):
        pltpu.make_async_copy(src, dst, recv_sems.at[S.load + k]).wait()

    def natural(kind, p, head):
        return kind * WIDTH + 192 * p + 64 * head

    def half_at(ref, column, high):
        tile = ref[:, column // 128 * 128 : column // 128 * 128 + 128]
        return tile if (column % 128 == 64) == high else pltpu.roll(tile, 64, 1)

    for p in range(4):
        for tile in range(5):
            pair = []
            for high in (0, 1):
                which = HALVES[2 * tile + high]
                pair.append(
                    jnp.zeros((24, 128), F32)
                    if which is None
                    else half_at(i_wqkv, natural(which[0], p, which[1]), bool(high))
                )
            r.wide_qkv[own24, 768 * p + 128 * tile : 768 * p + 128 * tile + 128] = jnp.where(
                low, pair[0], pair[1]
            )
        r.wide_qkv[own24, 768 * p + 640 : 768 * p + 768] = jnp.zeros((24, 128), F32)
    r.wide_in[own24, :] = i_win[...]
    r.wide_attn[own24, :] = i_wattn[...]
    r.w_out[z, c] = i_wout[...].astype(BF)
    r.toks[z] = i_tok[0]
    line_clear(r.r_out)
    line_clear(r.r_in)
    line_clear(r.d1r)
    for ref in (r.q_qkv, r.r_qkv):
        ref[:, :, PACK - HALF : HALF] = jnp.zeros((4, ref.shape[1], WIDTH - PACK), BF)
    lanes8 = lax.broadcasted_iota(jnp.int32, (8, 128), 1)
    half_cond = COND // 2
    speed = jnp.exp((lanes8 % half_cond).astype(F32) * (-math.log(10000.0) / half_cond))
    angle = r.when[0, 0].astype(F32) * speed
    wave = jnp.where(lanes8 < half_cond, jnp.cos(angle), jnp.sin(angle))
    r.conds_all[b] = wave * (1.0 / (1.0 + jnp.exp(-wave)))
    pl.semaphore_wait(barrier, ALL - 1)

    def token_block(k):
        return r.toks.at[k]

    def attn_block(k):
        return r.w_attn.at[pl.ds(pl.multiple_of(192 * b + 48 * k, 16), 48), part]

    def in_block(k):
        return r.w_in.at[:, k, :, part]

    def out_block(k):
        return r.w_out.at[k, c]

    peers(lambda k, to: push(r.conds_all.at[b], r.conds_all.at[b], S.cond, to, s))
    sent(S.cond, r.conds_all.at[0:3])
    push(r.wide_qkv.at[own24], r.wide_qkv.at[own24], S.mix_qkv, b, mate)
    sent(S.mix_qkv, r.wide_qkv.at[0:24])
    push(r.wide_attn.at[own24], r.wide_attn.at[own24], S.mix_attn, b, mate)
    sent(S.mix_attn, r.wide_attn.at[0:24])
    push(r.wide_in.at[own24], r.wide_in.at[own24], S.mix_in, b, mate)
    sent(S.mix_in, r.wide_in.at[0:24])

    got(S.cond, r.conds_all.at[0:3])
    row8 = lax.broadcasted_iota(jnp.int32, (8, 128), 0)
    cond4 = jnp.zeros((8, 128), F32)
    for k in range(4):
        cond4 = jnp.where(row8 == k, r.conds_all[k], cond4)
    o_conds[...] = cond4
    wide = i_wada.shape[0]
    r.mod_pad[...] = jnp.zeros((8, 384), F32)
    r.mod_pad[:, 0:wide] = dot_nt(cond4.astype(BF), i_wada[...].astype(BF))
    columns = pltpu.roll(r.mod_pad[...], lax.rem(wide * me, 128), 1)
    for k in range(4):
        for t in range(3):
            r.mod_send[k, t : t + 1, :] = columns[k : k + 1, 128 * t : 128 * t + 128]
        r.mod_send[k, 3:4, :] = jnp.zeros((1, 128), F32)

    def send_mod(k):
        other = lax.rem(me + k, ALL)
        ob = lax.div(other, SEQ)
        push(r.mod_send.at[ob], r.mod_got.at[me], S.mod, ob, lax.rem(other, SEQ))

    loop(ALL, send_mod, 1)
    sent(S.mod, r.mod_got.at[0:31])
    keep(r.mod_send.at[b], r.mod_got.at[me], S.mod)

    def block(src, first):
        return src.at[:, pl.ds(pl.multiple_of(first, 128), HALF)]

    def slices_along_line():
        def send(columns, width):
            def rows(to):
                first = pl.multiple_of(WIDTH * to + columns.start, 128)
                return r.s_qkv.at[:, pl.ds(first, width)]

            dst = r.w_qkv.at[chip_rows, columns]
            stack(lambda to: push(rows(to), dst, S.w_qkv, b, 2 * to + c))
            keep(rows(z), dst, S.w_qkv)

        by_core(send)
        sent_by_core(S.w_qkv, lambda width: r.w_qkv.at[0:144, 0:width])

    def over_plane(dst, at):
        rows = dst.at[group_rows, part]
        peers(lambda k, to: push(rows, rows, at + k, to, s))
        for k in (1, 2, 3):
            sent(at + k, dst.at[0:192, 0:HALF])

    def share(dst, at, onward):
        for k in range(4):
            rows = dst.at[pl.ds(pl.multiple_of(192 * near[k], 16), 192), part]
            if k:
                got(at + k, rows)
            push(rows, rows, onward, b, mate)
        sent(onward, dst.at[:, 0:HALF])

    def line_share(block, at, onward):
        for k in range(4):
            line_got(block, at, k)
            push(block(k), block(k), onward, b, mate)

    got(S.mix_qkv, r.wide_qkv.at[0:24])
    r.s_qkv[...] = r.wide_qkv[...].astype(BF)
    slices_along_line()
    line_gather(token_block, S.tok, rest=False)
    sent(S.tok, r.toks.at[0:3])
    got(S.mix_attn, r.wide_attn.at[0:24])
    r.s_attn[...] = r.wide_attn[...].astype(BF)

    def qkv_over_plane(columns, width):
        got(S.w_qkv, r.w_qkv.at[0:192, 0:width])
        rows = r.w_qkv.at[group_rows, columns]
        peers(lambda k, to: push(rows, rows, S.group_qkv + k, to, s))

    by_core(qkv_over_plane)
    for k in (1, 2, 3):
        sent_by_core(S.group_qkv + k, lambda width: r.w_qkv.at[0:192, 0:width])
    line_gather(token_block, S.tok, near=False)
    for h in range(2):

        @pl.when(c == h)
        def _():
            r.w_attn[chip_rows, 384 * h : 384 * h + 384] = r.s_attn[:, 384 * h : 384 * h + 384]

    line_gather(attn_block, S.w_attn)
    sent(S.w_attn, r.w_attn.at[0:144, 0:HALF])
    line_gather(out_block, S.w_out)
    sent(S.w_out, r.w_out.at[0:3, 0])
    got(S.mix_in, r.wide_in.at[0:24])
    r.s_in[...] = r.wide_in[...].astype(BF)
    peers(
        lambda k, to: push(
            block(r.s_in, WIDTH * to + HALF * c), r.w_in.at[b, z, :, part], S.plane_in, to, s
        )
    )
    keep(block(r.s_in, WIDTH * b + HALF * c), r.w_in.at[b, z, :, part], S.plane_in)
    sent(S.plane_in, r.w_in.at[0:3, 0, :, 0:HALF])

    def hidden_rows(k):
        place = (2 * k + c) * ROWS + lax.broadcasted_iota(jnp.int32, (ROWS, 1), 0)
        return (place >= r.when[1, 0]) & (place < r.when[1, 0] + r.when[2, 0])

    def first_norm(tokens, k):
        x0 = jnp.where(hidden_rows(k), i_vec[8:9, :], tokens.astype(F32))
        normed, inverse = normalize(x0)
        r.n1[k] = normed
        r.inv1[k] = jnp.broadcast_to(inverse, (ROWS, 128))
        return x0

    r.x0[...] = first_norm(i_tok[0], z)

    got(S.mod, r.mod_got)
    r.mod_flat[...] = jnp.zeros((40, 128), F32)
    for k in range(ALL):
        first = 9 * k // 8
        r.mod_flat[first : first + 3, :] += r.mod_got[k, 0:3, :]
    for k in range(6):
        row = jnp.concatenate(
            [r.mod_flat[6 * k + t : 6 * k + t + 1, :] for t in range(6)], axis=1
        )
        r.mod[k : k + 1, :] = row + i_vec[2 + k : 3 + k, :]

    def mod(k):
        return r.mod[k : k + 1, :]

    def vec(k):
        return i_vec[k : k + 1, :]

    r.h1[z] = (r.n1[z] * vec(0) * (1.0 + mod(1)) + mod(0)).astype(BF)
    r.dm[0] = (i_cot[0].astype(F32) * mod(5)).astype(BF)
    peers(lambda k, to: push(r.dm.at[0], r.dm.at[k], S.dm + k, to, s))
    for k in (1, 2, 3):
        sent(S.dm + k, r.dm.at[0])

    lanes = lax.broadcasted_iota(jnp.int32, (ROWS, 128), 1)
    first_half = lanes % HD < HD // 2
    speed = jnp.exp((lanes % (HD // 2)).astype(F32) * (-math.log(10000.0) / (HD // 2)))
    row = lax.broadcasted_iota(jnp.int32, (ROWS, 128), 0)

    def table(k):
        angle = ((2 * k + c) * ROWS + row).astype(F32) * speed
        r.turn[0, k] = jnp.cos(angle)
        sine = jnp.sin(angle)
        r.turn[1, k] = jnp.where(first_half, -sine, sine)

    loop(LINE, table)

    line_relay(token_block, S.tok)

    def qkv_share(columns, width):
        for k in range(4):
            rows = r.w_qkv.at[pl.ds(pl.multiple_of(192 * near[k], 16), 192), columns]
            if k:
                got(S.group_qkv + k, rows)
            push(rows, rows, S.fw_qkv, b, mate)

    by_core(qkv_share)
    sent_by_core(S.fw_qkv, lambda width: r.w_qkv.at[:, 0:width])
    by_core(lambda columns, width: got(S.fw_qkv, r.w_qkv.at[:, 0 : PACK - width]))
    for k in range(5):
        columns = slice(128 * k, 128 * k + 128)
        r.t_w_qkv[columns, :] = r.w_qkv[:, columns].T

    def turned(tile, sign, k):
        other = jnp.where(first_half, pltpu.roll(tile, 96, 1), pltpu.roll(tile, 32, 1))
        return tile * r.turn[0, k] + sign * (other * r.turn[1, k])

    def project(j):
        k = lax.rem(z + j, LINE)

        @pl.when(j > 0)
        def _():
            line_got(token_block, S.tok, k)
            first_norm(r.toks[k], k)
            r.h1[k] = (r.n1[k] * vec(0) * (1.0 + mod(1)) + mod(0)).astype(BF)

        x = dot(r.h1[k], r.w_qkv[:, 0:PACK])
        tiles = [x[:, 128 * t : 128 * t + 128] for t in range(5)]
        tiles[0] = turned(tiles[0], 1.0, k) * 0.125
        tiles[1] = jnp.where(low, turned(tiles[1], 1.0, k) * 0.125, tiles[1])
        tiles[2] = turned(tiles[2], 1.0, k)
        tiles[3] = turned(tiles[3], 1.0, k)
        for t in range(5):
            r.xb[0, k, :, 128 * t : 128 * t + 128] = tiles[t].astype(BF)
        push(r.xb.at[0, k], r.xb.at[1, k], S.xf + k, b, mate)

    loop(4, project)
    line_relay(attn_block, S.w_attn)
    for k in range(4):
        line_got(attn_block, S.w_attn, k)
    over_plane(r.w_attn, S.group_attn)
    for k in range(4):
        sent(S.xf + k, r.xb.at[0, 0])

    for k in range(6):
        columns = slice(128 * k, 128 * k + 128)
        r.t_h1[columns, :] = r.h1[:, :, columns].reshape(512, 128).T
    for k in range(4):
        got(S.xf + k, r.xb.at[0, 0])

    def tile_of(t):
        return r.xb[:, :, :, 128 * t : 128 * t + 128].reshape(1024, 128)

    heads = ((0, 2, 4, True, True), (0, 2, 4, False, False), (1, 3, 1, True, False))

    def queries(head, first, size):
        q_tile, _, _, q_low, _ = heads[head]
        q = r.xb[0, first : first + size, :, 128 * q_tile : 128 * q_tile + 128]
        return jnp.where(low if q_low else ~low, q.reshape(size * 128, 128), jnp.zeros((), BF))

    r.vt[0] = tile_of(4).T
    r.vt[1] = tile_of(1).T
    for half in range(2):
        at = slice(256 * half, 256 * half + 256)
        for head in range(3):
            scores = dot_nt(tile_of(heads[head][1]), queries(head, 2 * half, 2))
            weights = jnp.exp(scores - jnp.max(scores, axis=0, keepdims=True))
            weights = weights * (1.0 / jnp.sum(weights, axis=0, keepdims=True))
            weights = weights.astype(BF)
            r.pt[head, :, at] = weights
            out = dot(r.vt[head // 2], weights)
            if head == 0:
                r.ot[0, 0:64, at] = out[0:64]
            elif head == 1:
                r.ot[0, 64:128, at] = out[64:128]
            else:
                r.ot[1, 0:64, at] = out[64:128]
                r.ot[1, 64:128, at] = jnp.zeros((64, 256), F32)
        for k in (2 * half, 2 * half + 1):
            across = slice(128 * k, 128 * k + 128)
            r.os[k, 0:128, :] = r.ot[0, :, across].T.astype(BF)
            third = r.ot[1, 0:64, across]
            third = jnp.concatenate([third, pltpu.roll(third, 64, 1)], axis=0)
            r.os[k, 128:192, :] = third.T[0:64].astype(BF)
        for to in (2 * half, 2 * half + 1):

            @pl.when(z == to)
            def _():
                keep(r.os.at[to], r.ob.at[z], S.o)

            @pl.when(z != to)
            def _():
                push(r.os.at[to], r.ob.at[z], S.o, b, 2 * to + c)

        if half == 0:
            line_relay(out_block, S.w_out)

    sent(S.o, r.os.at[0:3])
    got(S.plane_in, r.w_in.at[:, 0, :, 0:HALF])
    line_gather(in_block, S.w_in)
    sent(S.w_in, r.w_in.at[0:3, :, :, 0:HALF])
    for k in range(2):
        r.kt[k] = tile_of(2 + k).T
    share(r.w_attn, S.group_attn, S.fw_attn)
    got(S.fw_attn, r.w_attn.at[:, 0:HALF])
    for p in range(4):
        first = 192 * p
        r.t_w_attn[:, 256 * p : 256 * p + 128] = r.w_attn[first : first + 128, :].T
        third = r.w_attn[first + 128 : first + 192, :]
        r.t_w_attn[:, 256 * p + 128 : 256 * p + 256] = jnp.concatenate(
            [third, jnp.zeros_like(third)], axis=0
        ).T
    got(S.o, r.ob)
    a = jnp.zeros((ROWS, WIDTH), F32)
    for p in range(4):
        third = r.ob[p, 128:192, :].astype(F32)
        third = jnp.concatenate([third, pltpu.roll(third, 64, 1)], axis=0)
        r.o2[p] = jnp.where(low, third, 0.0).astype(BF)
        a += dot(r.ob[p, 0:128, :], r.w_attn[192 * p : 192 * p + 128, :])
        a += dot(r.o2[p, :, 0:64], r.w_attn[192 * p + 128 : 192 * p + 192, :])
    r.a[...] = a
    x1 = r.x0[...] + mod(2) * a
    r.x1[...] = x1
    n2, inv2 = normalize(x1)
    r.n2[...] = n2
    r.inv2[...] = jnp.broadcast_to(inv2, (ROWS, 128))
    r.h2[0] = (n2 * vec(1) * (1.0 + mod(4)) + mod(3)).astype(BF)
    peers(lambda k, to: push(r.h2.at[0], r.h2.at[k], S.h2 + k, to, s))
    for k in (1, 2, 3):
        sent(S.h2 + k, r.h2.at[0])
    line_relay(in_block, S.w_in)
    line_share(out_block, S.w_out, S.fw_out)
    sent(S.fw_out, r.w_out.at[:, 0])
    got(S.fw_out, r.w_out.at[:, 0])

    for k in range(6):
        columns = slice(128 * k, 128 * k + 128)
        r.t_w_out[columns, :] = r.w_out[:, :, :, columns].reshape(WIDTH, 128).T

    def feed_back(k):
        @pl.when(k > 0)
        def _():
            got(S.dm + k, r.dm.at[0])

        r.back[k] = dot(r.dm[k], r.t_w_out[...])

    loop(4, feed_back)
    line_share(in_block, S.w_in, S.fw_in)
    sent(S.fw_in, r.w_in.at[:, :, :, 0:HALF])
    got(S.fw_in, r.w_in.at[:, :, :, 0:HALF])
    for k in range(6):
        columns = slice(128 * k, 128 * k + 128)
        r.t_w_in[columns, :] = r.w_in[:, :, :, columns].reshape(WIDTH, 128).T

    def feed(first, count):
        at = slice(first, first + count)
        size = count * ROWS
        u = dot(r.h2[at].reshape(size, WIDTH), r.w_in[...].reshape(WIDTH, WIDTH))
        slope = 0.7978845608028654
        cube = 0.044715
        t = jnp.tanh(slope * (u + cube * u * u * u))
        r.gb[at] = (0.5 * u * (1.0 + t)).astype(BF).reshape(count, ROWS, WIDTH)
        bend = 0.5 * (1.0 + t) + 0.5 * u * (1.0 - t * t) * (slope * (1.0 + 3.0 * cube * u * u))
        du = (r.back[at].reshape(size, WIDTH) * bend).astype(BF)
        r.du[at] = du.reshape(count, ROWS, WIDTH)
        r.dhs[at] = dot(du, r.t_w_in[...]).astype(BF).reshape(count, ROWS, WIDTH)

    feed(0, 1)
    for first, count in ((1, 2), (3, 1)):
        for k in range(first, first + count):
            got(S.h2 + k, r.h2.at[0])
        feed(first, count)
        for k in range(first, first + count):
            slot, to = toward(k)
            push(r.dhs.at[slot], r.dhr.at[slot], S.dh2, to, s)
    sent(S.dh2, r.dhs.at[0:3])
    def gather(own, others):
        total = own[0].astype(F32)
        for k in (1, 2, 3):
            total += others[k].astype(F32)
        return total

    for k in range(2):
        rows = slice(384 * k, 384 * k + 384)
        result = dot_tn(r.gb[:, :, rows].reshape(512, 384), r.dm[...].reshape(512, 768))
        r.g_out[2 * k : 2 * k + 2] = result.astype(BF).reshape(2, 2, 96, 768)
    push(r.g_out.at[:, 1 - c], r.p_out, S.pair_out, b, mate)
    sent(S.pair_out, r.p_out)

    def to_mate(grad, dst, at):
        push(grad.at[1 - c], dst, at, b, mate)
        sent(at, dst)

    def pair_sum(grad, pair, at):
        got(at, pair)
        grad[c] = (grad[c].astype(F32) + pair[...].astype(F32)).astype(BF)

    def plane_sum(grad, dst, at, packed=False):
        def send(columns, width):
            def rows(to):
                return grad.at[c, pl.ds(pl.multiple_of(192 * to, 16), 192), 0:width]

            peers(lambda k, to: push(rows(to), dst.at[k, :, 0:width], at, to, s))
            keep(rows(b), dst.at[0, :, 0:width], at)

        if packed:
            by_core(send)
            sent_by_core(at, lambda width: dst.at[0:3, :, 0:width])
        else:
            send(None, HALF)
            sent(at, dst.at[0:3])

    def line_sum(src, total, dst, first, at, packed=False):
        def send(columns, width):
            got(first, src.at[:, :, 0:width])
            total[...] = (
                (src[0].astype(F32) + src[1].astype(F32))
                + (src[2].astype(F32) + src[3].astype(F32))
            ).astype(BF)

            def rows(to):
                return total.at[pl.ds(pl.multiple_of(48 * to, 16), 48), 0:width]

            stack(lambda to: push(rows(to), dst.at[z, :, 0:width], at, b, 2 * to + c))
            keep(rows(z), dst.at[z, :, 0:width], at)

        if packed:
            by_core(send)
            sent_by_core(at, lambda width: dst.at[0:3, :, 0:width])
        else:
            send(None, HALF)
            sent(at, dst.at[0:3])

    def trade(total, final, at):
        push(total.at[:, mate24], final.at[:, c], at, b, mate)
        sent(at, final.at[:, 0])
        final[:, c] = total[:, own24, :]

    def in_product(k):
        rows = slice(384 * k, 384 * k + 384)
        result = dot_tn(r.h2[:, :, rows].reshape(512, 384), r.du[...].reshape(512, 768)).astype(BF)
        for h in range(2):
            r.g_in[h, 2 * k : 2 * k + 2] = result[:, 384 * h : 384 * h + 384].reshape(2, 4, 48, 384)

    in_product(0)

    got(S.pair_out, r.p_out)
    for k in range(4):
        r.g_out[k, c] = (r.g_out[k, c].astype(F32) + r.p_out[k].astype(F32)).astype(BF)

    def out_rows(k):
        return r.g_out.at[k, c]

    for j in (0, 1):
        line_add(j, out_rows, r.r_out, r.via_out, S.line_out)
    in_product(1)
    to_mate(r.g_in, r.p_in, S.pair_in)

    def add_out():
        k = line_order(2)
        r.g_out[k, c] = (r.g_out[k, c].astype(F32) + r.via_out[...].astype(F32)).astype(BF)

    got(S.dh2, r.dhr.at[0:3])
    dh = gather(r.dhs, r.dhr)
    n2 = r.n2[...]
    inv2 = r.inv2[:, 0:1]
    r.early[...] = jnp.zeros((8, 768), F32)
    r.early[2:3, :] = jnp.sum(dh, axis=0, keepdims=True)
    both = jnp.sum(dh * n2, axis=0, keepdims=True)
    r.early[3:4, :] = both * vec(1)
    r.early[0:1, :] = both * (1.0 + mod(4))
    grad = dh * ((1.0 + mod(4)) * vec(1))
    dx1 = i_cot[0].astype(F32) + norm_back(n2, inv2, grad)
    r.dx1[...] = dx1
    r.early[1:2, :] = jnp.sum(dx1 * r.a[...], axis=0, keepdims=True)
    r.das[...] = (dx1 * mod(2)).astype(BF)
    for p in range(4):
        result = dot(r.das[...], r.t_w_attn[:, 256 * p : 256 * p + 256])
        r.dos[p, 0:128, :] = result[:, 0:128].astype(BF)
        third = result[:, 128:256]
        third = jnp.where(low, third[0:64], pltpu.roll(third[64:128], 64, 1))
        r.dos[p, 128:192, :] = third.astype(BF)
    stack(lambda to: push(r.dos.at[to], r.dob.at[z], S.do, b, 2 * to + c))
    keep(r.dos.at[z], r.dob.at[z], S.do)
    sent(S.do, r.dos.at[0:3])
    for t in range(3):
        at = slice(256 * t, 256 * t + 256)
        mm = dot(r.gb[...].reshape(512, WIDTH), r.w_out[:, :, :, at].reshape(WIDTH, 256))
        r.mms[:, :, at] = mm.astype(BF).reshape(4, ROWS, 256)
    peers(lambda k, to: push(r.mms.at[k], r.mmr.at[k], S.mm, to, s))
    sent(S.mm, r.mms.at[0:3])

    for p in range(4):
        for rows, left_side in (
            (slice(192 * p, 192 * p + 128), r.ob[p, 0:128, :]),
            (slice(192 * p + 128, 192 * p + 192), r.o2[p]),
        ):
            result = dot_tn(left_side, r.das[...])[0 : rows.stop - rows.start].astype(BF)
            r.g_attn[0, rows, :] = result[:, 0:HALF]
            r.g_attn[1, rows, :] = result[:, HALF:WIDTH]
    to_mate(r.g_attn, r.p_attn, S.pair_attn)

    def small_sum(src, pair, line, plane, whole, at):
        def first():
            push(src, pair, at, b, mate)
            sent(at, src)

        def second():
            got(at, pair)
            total = src[...] + pair[...]
            line[z] = (1 - c) * total[:, 0:HALF] + c * total[:, HALF:WIDTH]
            stack(lambda to: push(line.at[z], line.at[z], at + 1, b, 2 * to + c))
            sent(at + 1, line.at[0:3])

        def third():
            got(at + 1, line.at[0:3])
            plane[b] = (line[0] + line[1]) + (line[2] + line[3])
            peers(lambda k, to: push(plane.at[b], plane.at[b], at + 2, to, s))
            sent(at + 2, plane.at[0:3])

        def fourth():
            got(at + 2, plane.at[0:3])
            whole[c] = plane[...]
            push(plane, whole.at[c], at + 3, b, mate)
            sent(at + 3, plane)

        def rows(k):
            return jnp.concatenate([whole[0, k], whole[1, k]], axis=1)

        return first, second, third, fourth, rows

    early_steps = small_sum(
        r.early, r.early_pair, r.early_line, r.early_plane, r.early_all, S.early
    )
    late_steps = small_sum(r.late, r.late_pair, r.late_line, r.late_plane, r.late_all, S.late)

    pair_sum(r.g_in, r.p_in, S.pair_in)
    line_via(r.via_out, S.line_out, add_out)
    for j in (2, 3):
        line_add(j, out_rows, r.r_out, r.via_out, S.line_out)
    sent(S.line_out, r.r_out.at[0:3])

    def in_rows(k):
        return r.g_in.at[c, :, k]

    for j in (0, 1):
        line_add(j, in_rows, r.r_in, r.via_in, S.line_in)

    def add_in():
        k = line_order(2)
        r.g_in[c, :, k] = (r.g_in[c, :, k].astype(F32) + r.via_in[...].astype(F32)).astype(BF)

    pair_sum(r.g_attn, r.p_attn, S.pair_attn)
    plane_sum(r.g_attn, r.q_attn, S.plane_attn)

    got(S.do, r.dob)
    dot0 = r.dob[:, 0:128, :].reshape(512, 128)
    third = r.dob[:, 128:192, :].astype(F32).reshape(256, 128)
    other_rows = jnp.where(low, pltpu.roll(third, 64, 1), 0.0).reshape(4, 64, 128)
    third = jnp.where(low, third, 0.0).reshape(4, 64, 128)
    dot1 = jnp.concatenate([third, other_rows], axis=1).reshape(512, 128)
    zero = jnp.zeros((), BF)
    moved = pltpu.roll(dot1, 64, 1).astype(BF)
    grads = (jnp.where(low, dot0, zero), jnp.where(low, zero, dot0), moved)
    product = dot0.astype(F32).T * r.ot[0]
    deltas = (
        jnp.sum(product[0:64], axis=0, keepdims=True),
        jnp.sum(product[64:128], axis=0, keepdims=True),
        jnp.sum(dot1.T * r.ot[1], axis=0, keepdims=True),
    )
    for head in range(3):
        values = tile_of(heads[head][2])
        for half in range(2):
            at = slice(256 * half, 256 * half + 256)
            dp = dot_nt(values, grads[head][at])
            r.dst[head, :, at] = (
                r.pt[head, :, at].astype(F32) * (dp - deltas[head][:, at])
            ).astype(BF)

    def key_grads(rows):
        dk = [dot(r.dst[head, rows, :], queries(head, 0, 4)) for head in range(3)]
        dv = [dot(r.pt[head, rows, :], grads[head]) for head in range(3)]
        return (dv[2], dk[0] + dk[1], dk[2], dv[0] + dv[1])

    for t, tile in enumerate(key_grads(slice(512, 1024))):
        r.gps[:, 128 * t : 128 * t + 128] = tile.astype(BF)
    push(r.gps, r.gpr, S.gp, b, mate)
    sent(S.gp, r.gps)
    for t, tile in enumerate(key_grads(slice(0, 512))):
        r.ga[:, 128 * t + 128 : 128 * t + 256] = tile
    for half in range(2):
        at = slice(256 * half, 256 * half + 256)
        turned_q = [dot(r.kt[head // 2], r.dst[head, :, at]) for head in range(3)]
        top = jnp.concatenate([turned_q[0][0:64], turned_q[1][64:128]], axis=0)
        r.ga[at, 0:128] = top.T * 0.125
        r.ga[at, 128:256] += turned_q[2].T * 0.125
    line_via(r.via_in, S.line_in, add_in)
    for j in (2, 3):
        line_add(j, in_rows, r.r_in, r.via_in, S.line_in)
    sent(S.line_in, r.r_in.at[0:3])
    got(S.gp, r.gpr)

    def dh1_rows(k):
        return r.d1s.at[k]

    def back_turn(k):
        rows = pl.ds(pl.multiple_of(128 * k, 128), 128)
        tiles = [r.ga[rows, 0:128]] + [
            r.ga[rows, 128 * t : 128 * t + 128]
            + r.gpr[rows, 128 * t - 128 : 128 * t].astype(F32)
            for t in range(1, 5)
        ]
        tiles[0] = turned(tiles[0], -1.0, k)
        tiles[1] = jnp.where(low, turned(tiles[1], -1.0, k), tiles[1])
        tiles[2] = turned(tiles[2], -1.0, k)
        tiles[3] = turned(tiles[3], -1.0, k)
        for t in range(5):
            r.dqkv[k, :, 128 * t : 128 * t + 128] = tiles[t].astype(BF)
        r.dqkv[k, :, PACK:WIDTH] = jnp.zeros((128, 128), BF)

    back_turn(line_order(0))

    def unproject(j):
        k = line_order(j)
        partial_sum = dot(r.dqkv[k, :, 0:PACK], r.t_w_qkv[...])
        r.d1s[k] = partial_sum.astype(BF)
        if j == 2:

            def add():
                r.d1s[k] = (partial_sum + r.via_dh1[...].astype(F32)).astype(BF)

            line_via(r.via_dh1, S.dh1, add)
        line_add(j, dh1_rows, r.d1r, r.via_dh1, S.dh1)
        n = r.n1[k]
        e = partial_sum * ((1.0 + mod(1)) * vec(0))
        weight = jnp.where(hidden_rows(k), r.inv1[k][:, 0:1], 0.0)
        centred = (
            e
            - jnp.mean(e, axis=-1, keepdims=True)
            - n * jnp.mean(e * n, axis=-1, keepdims=True)
        )
        r.late[0:1, :] += jnp.sum(partial_sum * n, axis=0, keepdims=True)
        r.late[1:2, :] += jnp.sum(partial_sum, axis=0, keepdims=True)
        r.late[3:4, :] += jnp.sum(weight * centred, axis=0, keepdims=True)

    r.late[...] = jnp.zeros((4, 768), F32)
    r.late[3:4, :] = jnp.sum(
        jnp.where(hidden_rows(z), r.dx1[...], 0.0), axis=0, keepdims=True
    )
    unproject(0)
    for j in (1, 2, 3):
        back_turn(line_order(j))

    def qkv_rows(k):
        rows = pl.ds(pl.multiple_of(128 * k, 128), 128)
        result = dot(r.t_h1[rows, :], r.dqkv[...].reshape(512, WIDTH)).astype(BF)
        r.g_qkv[0, rows, :] = result[:, 0:HALF]
        r.g_qkv[1, rows, :] = result[:, HALF:WIDTH]

    loop(6, qkv_rows)
    to_mate(r.g_qkv, r.p_qkv, S.pair_qkv)
    unproject(1)
    pair_sum(r.g_qkv, r.p_qkv, S.pair_qkv)
    plane_sum(r.g_qkv, r.q_qkv, S.plane_qkv, True)
    got(S.mm, r.mmr.at[0:3])
    mm = gather(r.mms, r.mmr)
    o_y[...] = (r.x1[...] + mod(5) * mm).astype(BF)
    r.early[4:5, :] = jnp.sum(i_cot[0].astype(F32) * mm, axis=0, keepdims=True)
    early_steps[0]()
    unproject(2)
    unproject(3)
    sent(S.dh1, r.d1s.at[0:3])
    both = r.late[0:1, :]
    r.late[2:3, :] = both * vec(0)
    r.late[0:1, :] = both * (1.0 + mod(1))
    late_steps[0]()
    early_steps[1]()
    line_sum(r.q_attn, r.m_attn, r.r_attn, S.plane_attn, S.line_attn)
    late_steps[1]()

    line_done(r.r_in, S.line_in)
    r.m_in[...] = (
        (r.r_in[0].astype(F32) + r.r_in[1].astype(F32))
        + (r.r_in[2].astype(F32) + r.r_in[3].astype(F32))
    ).astype(BF)
    peers(lambda k, to: push(r.m_in.at[to], r.u_in.at[b], S.slice_in, to, s))
    keep(r.m_in.at[b], r.u_in.at[b], S.slice_in)
    sent(S.slice_in, r.u_in.at[0:3])
    line_sum(r.q_qkv, r.m_qkv, r.r_qkv, S.plane_qkv, S.line_qkv, True)
    early_steps[2]()
    late_steps[2]()

    line_done(r.d1r, S.dh1)
    dh = (r.d1r[0].astype(F32) + r.d1r[1].astype(F32)) + (
        r.d1r[2].astype(F32) + r.d1r[3].astype(F32)
    )
    n1 = r.n1[z]
    grad = dh * ((1.0 + mod(1)) * vec(0))
    dx0 = r.dx1[...] + norm_back(n1, r.inv1[z][:, 0:1], grad)
    o_dx[...] = jnp.where(hidden_rows(z), 0.0, dx0)
    early_steps[3]()
    late_steps[3]()

    line_done(r.r_out, S.line_out)
    total = (r.r_out[0].astype(F32) + r.r_out[1].astype(F32)) + (
        r.r_out[2].astype(F32) + r.r_out[3].astype(F32)
    )
    o_gout[...] = total
    squares = total * total
    squares = jnp.sum(squares[:, 0:128] + squares[:, 128:256] + squares[:, 256:384]
                      + squares[:, 384:512] + squares[:, 512:640] + squares[:, 640:768],
                      axis=0, keepdims=True)

    def fold(value):
        total = value[:, 0:128] * value[:, 0:128]
        for t in range(1, value.shape[1] // 128):
            total += value[:, 128 * t : 128 * t + 128] * value[:, 128 * t : 128 * t + 128]
        return jnp.sum(total, axis=0, keepdims=True)

    got(S.slice_in, r.u_in)
    r.t_in[...] = r.u_in[...].astype(F32)
    for p in range(4):
        squares += fold(r.t_in[p])
    trade(r.t_in, r.f_in, S.last_in)
    got(S.line_attn, r.r_attn)
    r.t_attn[0] = (r.r_attn[0].astype(F32) + r.r_attn[1].astype(F32)) + (
        r.r_attn[2].astype(F32) + r.r_attn[3].astype(F32)
    )
    squares += fold(r.t_attn[0])
    trade(r.t_attn, r.f_attn, S.last_attn)
    by_core(lambda columns, width: got(S.line_qkv, r.r_qkv.at[:, :, 0:width]))
    r.t_qkv[...] = r.r_qkv[...].astype(F32)
    trade(r.t_qkv, r.f_qkv, S.last_qkv)
    for p in range(4):
        squares += fold(r.t_qkv[p])
    r.sq[me] = squares

    def send_sq(k):
        other = lax.rem(me + k, ALL)
        push(r.sq.at[me], r.sq.at[me], S.sq, lax.div(other, SEQ), lax.rem(other, SEQ))

    loop(ALL, send_sq, 1)
    sent(S.sq, r.sq.at[0:31])
    got(S.last_in, r.f_in.at[:, 0])
    got(S.last_attn, r.f_attn.at[:, 0])
    for h in range(2):
        for p in range(4):
            value = r.f_in[p, h]
            o_gin[:, 768 * p + 384 * h : 768 * p + 384 * h + 384] = value
        value = r.f_attn[0, h]
        o_gattn[:, 384 * h : 384 * h + 384] = value
    got(S.last_qkv, r.f_qkv.at[:, 0])
    where = {which: index for index, which in enumerate(HALVES) if which is not None}

    def packed_half(chunk, high):
        kind, rest = chunk // 12, chunk % 12
        index = where[(kind, rest % 3)]
        t = index // 2
        tile = r.f_qkv[rest // 3, t // 3, :, t % 3 * 128 : t % 3 * 128 + 128]
        return tile if index % 2 == high else pltpu.roll(tile, 64, 1)

    for t in range(18):
        o_gqkv[:, 128 * t : 128 * t + 128] = jnp.where(
            low, packed_half(2 * t, 0), packed_half(2 * t + 1, 1)
        )
    got(S.early + 3, r.early_all.at[0])
    got(S.late + 3, r.late_all.at[0])
    early_rows = [early_steps[4](k) for k in range(4)]
    late_rows = [late_steps[4](k) for k in range(4)]
    mods = []
    for k in range(4):
        early, late = early_rows[k], late_rows[k]
        rows = jnp.concatenate([late[1:3], early[1:5], jnp.zeros((2, 768), F32)], axis=0)
        for n in range(6):
            for m in range(6):
                r.dmod_flat[k, 6 * n + m : 6 * n + m + 1, :] = rows[
                    n : n + 1, 128 * m : 128 * m + 128
                ]
        mods.append(rows)
    gain = jnp.concatenate(
        [
            sum(late_rows[k][0:1] for k in range(4)),
            sum(early_rows[k][0:1] for k in range(4)),
            (mods[0] + mods[1] + mods[2] + mods[3])[0:6],
        ],
        axis=0,
    )
    mask_row = sum(late_rows[k][3:4] for k in range(4))
    gains = jnp.concatenate([gain, mask_row, jnp.zeros((7, 768), F32)], axis=0)
    masters = jnp.concatenate([i_vec[...], jnp.zeros((7, 768), F32)], axis=0)
    own = lax.rem(WIDTH - 24 * me, WIDTH)
    o_gvec[...] = pltpu.roll(gains, own, 1)[:, 0:128]
    o_vec[...] = pltpu.roll(masters, own, 1)[:, 0:128]
    r.mod_pad[...] = jnp.zeros((8, 384), F32)
    window = lax.div(wide * me, 128)
    for k in range(4):
        rows = r.dmod_flat[k, pl.ds(window, 3), :]
        for m in range(3):
            r.mod_pad[k : k + 1, 128 * m : 128 * m + 128] = rows[m : m + 1, :]
    o_dmod[...] = pltpu.roll(r.mod_pad[...], lax.rem(384 - lax.rem(wide * me, 128), 384), 1)[:, 0:256]
    small = jnp.sum(gain * gain) + jnp.sum(mask_row * mask_row)
    conds = [r.conds_all[k][0:1].astype(BF).astype(F32) for k in range(4)]
    for k in range(4):
        for m in range(k, 4):
            term = jnp.sum(mods[k] * mods[m]) * jnp.sum(conds[k] * conds[m])
            small += term if m == k else 2.0 * term
    got(S.sq, r.sq.at[0:31])
    total = r.sq[0]
    for k in range(1, ALL):
        total += r.sq[k]
    o_norm[...] = jnp.broadcast_to(jnp.sqrt(jnp.sum(total) + small), (8, 128))

    for drained in drains:
        drained()


def run_layer(*args):
    shapes = (
        ((ROWS, WIDTH), BF),
        ((ROWS, WIDTH), F32),
        ((8, 128), F32),
        ((24, 3 * WIDTH), F32),
        ((24, WIDTH), F32),
        ((24, 4 * WIDTH), F32),
        ((96, WIDTH), F32),
        ((8, 256), F32),
        ((16, 128), F32),
        ((16, 128), F32),
        ((8, 128), F32),
    )
    whole = pl.BlockSpec(memory_space=pltpu.VMEM)
    return pl.pallas_call(
        layer_kernel,
        out_shape=[jax.ShapeDtypeStruct(shape, kind) for shape, kind in shapes],
        in_specs=[pl.BlockSpec(memory_space=pl.ANY)] * len(args),
        out_specs=[whole] * len(shapes),
        scratch_shapes=[pltpu.VMEM(shape, kind) for shape, kind in SCRATCH.values()]
        + [pltpu.SMEM((3, 1), jnp.int32)]
        + [pltpu.SemaphoreType.DMA((SEM_COUNT,)), pltpu.SemaphoreType.DMA((SEM_COUNT,))],
        compiler_params=pltpu.CompilerParams(
            collective_id=0, has_side_effects=True, vmem_limit_bytes=60 * 1024 * 1024
        ),
    )(*args)


HELD = (2, 8, 9, 7, 10, 3, 4, 5, 6)


def finish_kernel(*refs):
    sources, outs, refs = refs[:28], refs[28:49], refs[49:]
    near, results, load_sems, store_sems = refs[:28], refs[28:46], refs[46], refs[47]
    norm, g_vec, own_vec, dmod, conds = near[:5]
    weights, moments = (own_vec, *near[9:14]), near[14:26]

    order = list(range(5)) + [14, 15, 9, 16, 17]
    for k in range(2, 6):
        order += [3 + k, 8 + k, 14 + 2 * k, 15 + 2 * k]
    loads = {}
    for n in order:
        source = sources[HELD[n]] if n < 9 else sources[n + 2]
        loads[n] = pltpu.make_async_copy(source, near[n], load_sems.at[n])
        loads[n].start()
    for n in (26, 27):
        loads[n] = pltpu.make_async_copy(sources[n - 26], near[n], load_sems.at[n])
        loads[n].start()
    for n in order[:10]:
        loads[n].wait()
    outs[2][0, 0] = norm[0, 0]
    clip = jnp.minimum(1.0, CLIP / (norm[0:1, 0:1] + 1e-06))
    wide, narrow = near[9].shape[0], moments[0].shape[1]
    rounded = conds[...].astype(BF).astype(F32)
    turned_mod = dmod[...].T
    g_ada = turned_mod[0:wide, 0:1] * rounded[0:1, :]
    for k in range(1, 4):
        g_ada += turned_mod[0:wide, k : k + 1] * rounded[k : k + 1, :]
    stores = []
    for k in range(6):
        if k > 1:
            for n in order[2 + 4 * k : 6 + 4 * k]:
                loads[n].wait()
        grad = g_vec[0:9, 0:narrow] if k == 0 else g_ada if k == 1 else near[3 + k][...]
        updated = adam_step(
            weights[k][...] if k else own_vec[0:9, 0:narrow],
            grad * clip,
            moments[2 * k][...],
            moments[2 * k + 1][...],
            RATE if k else RATE_VECTORS,
            DECAY if k else 0.0,
        )
        for n in range(3):
            at = 3 * k + n
            results[at][...] = updated[n]
            stores.append(pltpu.make_async_copy(results[at], outs[3 + at], store_sems.at[at]))
            stores[-1].start()
    for n in (26, 27):
        loads[n].wait()
        stores.append(pltpu.make_async_copy(near[n], outs[n - 26].at[0], store_sems.at[n - 8]))
        stores[-1].start()
    for copy in stores:
        copy.wait()


def run_finish(partial_results, weights, moments):
    shapes = [((1, ROWS, WIDTH), BF), ((1, ROWS, WIDTH), F32), ((1, 1), F32)]
    for moment in moments[::2]:
        shapes += [(moment.shape, F32)] * 3
    far = pl.BlockSpec(memory_space=pl.ANY)
    specs = [far] * len(shapes)
    specs[2] = pl.BlockSpec(memory_space=pltpu.SMEM)
    near = [partial_results[k] for k in HELD] + [*weights, *moments, *partial_results[:2]]
    args = (*partial_results, *weights, *moments)
    return pl.pallas_call(
        finish_kernel,
        out_shape=[jax.ShapeDtypeStruct(shape, kind) for shape, kind in shapes],
        in_specs=[far] * len(args),
        out_specs=specs,
        scratch_shapes=[pltpu.VMEM(array.shape, array.dtype) for array in near]
        + [pltpu.VMEM(shape, kind) for shape, kind in shapes[3:]]
        + [pltpu.SemaphoreType.DMA((28,)), pltpu.SemaphoreType.DMA((20,))],
        compiler_params=pltpu.CompilerParams(vmem_limit_bytes=60 * 1024 * 1024),
    )(*args)


def slices(
    tokens_in,
    cotangent,
    timesteps,
    span_start,
    span_len,
    vectors,
    w_ada,
    w_qkv,
    w_attn,
    w_in,
    w_out,
    m_vec,
    v_vec,
    m_ada,
    v_ada,
    m_qkv,
    v_qkv,
    m_attn,
    v_attn,
    m_in,
    v_in,
    m_out,
    v_out,
):
    partial_results = run_layer(
        timesteps,
        span_start,
        span_len,
        tokens_in,
        cotangent,
        vectors,
        w_ada.T,
        w_qkv,
        w_attn,
        w_in,
        w_out,
    )
    moments = (
        m_vec,
        v_vec,
        m_ada.T,
        v_ada.T,
        m_qkv,
        v_qkv,
        m_attn,
        v_attn,
        m_in,
        v_in,
        m_out,
        v_out,
    )
    results = run_finish(partial_results, (w_ada.T, w_qkv, w_attn, w_in, w_out), moments)
    ada_results = [result.T for result in results[6:9]]
    return (*results[:2], results[2].reshape(()), *results[3:6], *ada_results, *results[9:])


def solution(mesh):
    in_specs = (
        P("dp", "seq", None),
        P("dp", "seq", None),
        P("dp"),
        P("dp"),
        P("dp"),
        P(),
        P(None, ("dp", "seq")),
        P(("dp", "seq"), None),
        P(("dp", "seq"), None),
        P(("dp", "seq"), None),
        P(("dp", "seq"), None),
        P(None, ("dp", "seq")),
        P(None, ("dp", "seq")),
        P(None, ("dp", "seq")),
        P(None, ("dp", "seq")),
        P(("dp", "seq"), None),
        P(("dp", "seq"), None),
        P(("dp", "seq"), None),
        P(("dp", "seq"), None),
        P(("dp", "seq"), None),
        P(("dp", "seq"), None),
        P(("dp", "seq"), None),
        P(("dp", "seq"), None),
    )
    out_specs = (
        P("dp", "seq", None),
        P("dp", "seq", None),
        P(),
        P(None, ("dp", "seq")),
        P(None, ("dp", "seq")),
        P(None, ("dp", "seq")),
        P(None, ("dp", "seq")),
        P(None, ("dp", "seq")),
        P(None, ("dp", "seq")),
        P(("dp", "seq"), None),
        P(("dp", "seq"), None),
        P(("dp", "seq"), None),
        P(("dp", "seq"), None),
        P(("dp", "seq"), None),
        P(("dp", "seq"), None),
        P(("dp", "seq"), None),
        P(("dp", "seq"), None),
        P(("dp", "seq"), None),
        P(("dp", "seq"), None),
        P(("dp", "seq"), None),
        P(("dp", "seq"), None),
    )
    sizes = dict(mesh.shape)
    local = slices if (sizes["dp"], sizes["seq"]) == (4, 8) else plain
    return jax.shard_map(local, mesh=mesh, in_specs=in_specs, out_specs=out_specs, check_vma=False)
```

profile of v0, /device:TPU:0, one launch (start us, length us, event | category | flops | bytes accessed | tf_op | source)
XLA Modules:
  0.0 126.1 jit_solution(10923318410524880988)
XLA Ops:
  2.6 118.8 %shard_map.382 = (bf16[128,768]{1,0:T(8,128)(2,1)}, f32[128,768]{1,0:T(8,128)}, f32[8,128]{1,0:T(8,128)}, f32[24,2304]{1,0:T(8,128)}, f32[24,768]{1,0:T(8,128)},...) custom-call(s32[1]{0:T(128)S(6)} %copy.44.i_time, ...), custom_call_target="tpu_custom_call" | custom-call | tf_op jit(solution)/shard_map/pallas_call | solution.py:1637
  121.4 4.6 %shard_map.383 = (bf16[1,128,768]{2,1,0:T(8,128)(2,1)}, f32[1,128,768]{2,1,0:T(8,128)}, f32[1,1]{1,0:T(1,128)}, f32[9,24]{1,0:T(8,128)}, f32[9,24]{1,0:T(8,128)}...) custom-call(bf16[128,768]{1,0:T(8,128)(2,1)} %get-tuple-element.53.r, ...), custom_call_target="tpu_custom_call" | custom-call | tf_op jit(solution)/shard_map/pallas_call | solution.py:1717
where the time goes:
time: 126 us
  Pallas kernels  123 us (98%)
  between operations  2.78 us (2%)
    pallas_call x1, Pallas kernels, run_layer(): pl.pallas_call(layer_kernel, out_shape=[jax.ShapeDtypeStruct(shape, kind)...  119 us
    pallas_call x1, Pallas kernels, run_finish(): pl.pallas_call(finish_kernel, out_shape=[jax.ShapeDtypeStruct(shape, kind...  4.59 us

commit v1 on v0

--- a/solution.py
+++ b/solution.py
@@ -1279,13 +1279,20 @@
     r.dx1[...] = dx1
     r.early[1:2, :] = jnp.sum(dx1 * r.a[...], axis=0, keepdims=True)
     r.das[...] = (dx1 * mod(2)).astype(BF)
-    for p in range(4):
-        result = dot(r.das[...], r.t_w_attn[:, 256 * p : 256 * p + 256])
-        r.dos[p, 0:128, :] = result[:, 0:128].astype(BF)
+    def make_do(to):
+        columns = pl.ds(pl.multiple_of(256 * to, 256), 256)
+        result = dot(r.das[...], r.t_w_attn[:, columns])
+        r.dos[to, 0:128, :] = result[:, 0:128].astype(BF)
         third = result[:, 128:256]
         third = jnp.where(low, third[0:64], pltpu.roll(third[64:128], 64, 1))
-        r.dos[p, 128:192, :] = third.astype(BF)
-    stack(lambda to: push(r.dos.at[to], r.dob.at[z], S.do, b, 2 * to + c))
+        r.dos[to, 128:192, :] = third.astype(BF)
+
+    def send_do(to):
+        make_do(to)
+        push(r.dos.at[to], r.dob.at[z], S.do, b, 2 * to + c)
+
+    stack(send_do)
+    make_do(z)
     keep(r.dos.at[z], r.dob.at[z], S.do)
     sent(S.do, r.dos.at[0:3])
     for t in range(3):
@@ -1658,15 +1665,15 @@
     weights, moments = (own_vec, *near[9:14]), near[14:26]
 
     order = list(range(5)) + [14, 15, 9, 16, 17]
-    for k in range(2, 6):
+    for k in (4, 5, 2, 3):
         order += [3 + k, 8 + k, 14 + 2 * k, 15 + 2 * k]
     loads = {}
+    for n in (26, 27):
+        loads[n] = pltpu.make_async_copy(sources[n - 26], near[n], load_sems.at[n])
+        loads[n].start()
     for n in order:
         source = sources[HELD[n]] if n < 9 else sources[n + 2]
         loads[n] = pltpu.make_async_copy(source, near[n], load_sems.at[n])
-        loads[n].start()
-    for n in (26, 27):
-        loads[n] = pltpu.make_async_copy(sources[n - 26], near[n], load_sems.at[n])
         loads[n].start()
     for n in order[:10]:
         loads[n].wait()
@@ -1679,9 +1686,13 @@
     for k in range(1, 4):
         g_ada += turned_mod[0:wide, k : k + 1] * rounded[k : k + 1, :]
     stores = []
-    for k in range(6):
-        if k > 1:
-            for n in order[2 + 4 * k : 6 + 4 * k]:
+    for n in (26, 27):
+        loads[n].wait()
+        stores.append(pltpu.make_async_copy(near[n], outs[n - 26].at[0], store_sems.at[n - 8]))
+        stores[-1].start()
+    for step, k in enumerate((0, 1, 4, 5, 2, 3)):
+        if step > 1:
+            for n in order[2 + 4 * step : 6 + 4 * step]:
                 loads[n].wait()
         grad = g_vec[0:9, 0:narrow] if k == 0 else g_ada if k == 1 else near[3 + k][...]
         updated = adam_step(
@@ -1697,10 +1708,6 @@
             results[at][...] = updated[n]
             stores.append(pltpu.make_async_copy(results[at], outs[3 + at], store_sems.at[at]))
             stores[-1].start()
-    for n in (26, 27):
-        loads[n].wait()
-        stores.append(pltpu.make_async_copy(near[n], outs[n - 26].at[0], store_sems.at[n - 8]))
-        stores[-1].start()
     for copy in stores:
         copy.wait()
 

time: 126 us -> 126 us (level)
  no operation moved by 1% of the time
where the time goes in v1:
time: 126 us
  Pallas kernels  123 us (98%)
  between operations  2.78 us (2%)
    pallas_call x1, Pallas kernels, run_layer(): pl.pallas_call(layer_kernel, out_shape=[jax.ShapeDtypeStruct(shape, kind)...  119 us
    pallas_call x1, Pallas kernels, run_finish(): pl.pallas_call(finish_kernel, out_shape=[jax.ShapeDtypeStruct(shape, kind...  4.36 us

profile of v1, /device:TPU:0, one launch (start us, length us, event | category | flops | bytes accessed | tf_op | source)
XLA Modules:
  0.0 125.9 jit_solution(1487119551275227886)
XLA Ops:
  2.6 118.7 %shard_map.382 = (bf16[128,768]{1,0:T(8,128)(2,1)}, f32[128,768]{1,0:T(8,128)}, f32[8,128]{1,0:T(8,128)}, f32[24,2304]{1,0:T(8,128)}, f32[24,768]{1,0:T(8,128)},...) custom-call(s32[1]{0:T(128)S(6)} %copy.44.i_time, ...), custom_call_target="tpu_custom_call" | custom-call | tf_op jit(solution)/shard_map/pallas_call | solution.py:1644
  121.3 4.4 %shard_map.383 = (bf16[1,128,768]{2,1,0:T(8,128)(2,1)}, f32[1,128,768]{2,1,0:T(8,128)}, f32[1,1]{1,0:T(1,128)}, f32[9,24]{1,0:T(8,128)}, f32[9,24]{1,0:T(8,128)}...) custom-call(bf16[128,768]{1,0:T(8,128)(2,1)} %get-tuple-element.53.r, ...), custom_call_target="tpu_custom_call" | custom-call | tf_op jit(solution)/shard_map/pallas_call | solution.py:1724

commit v2 on v1

--- a/solution.py
+++ b/solution.py
@@ -429,6 +429,7 @@
     mix_in=1,
     mix_attn=1,
     mod=1,
+    mod_pair=1,
     w_qkv=1,
     w_attn=4,
     plane_in=1,
@@ -495,7 +496,7 @@
     t_h1=((768, 512), BF),
     conds_all=((4, 8, 128), F32),
     mod_send=((4, 4, 128), F32),
-    mod_got=((32, 4, 128), F32),
+    mod_got=((2, 16, 4, 128), F32),
     mod_flat=((40, 128), F32),
     mod_pad=((8, 384), F32),
     turn=((2, 4, 128, 128), F32),
@@ -871,13 +872,13 @@
         r.mod_send[k, 3:4, :] = jnp.zeros((1, 128), F32)
 
     def send_mod(k):
-        other = lax.rem(me + k, ALL)
-        ob = lax.div(other, SEQ)
-        push(r.mod_send.at[ob], r.mod_got.at[me], S.mod, ob, lax.rem(other, SEQ))
-
-    loop(ALL, send_mod, 1)
-    sent(S.mod, r.mod_got.at[0:31])
-    keep(r.mod_send.at[b], r.mod_got.at[me], S.mod)
+        other = lax.rem(chip + k, CHIPS)
+        ob = lax.div(other, LINE)
+        push(r.mod_send.at[ob], r.mod_got.at[c, chip], S.mod, ob, 2 * lax.rem(other, LINE) + c)
+
+    loop(CHIPS, send_mod, 1)
+    sent(S.mod, r.mod_got.at[0, 0:15])
+    keep(r.mod_send.at[b], r.mod_got.at[c, chip], S.mod)
 
     def block(src, first):
         return src.at[:, pl.ds(pl.multiple_of(first, 128), HALF)]
@@ -964,11 +965,14 @@
 
     r.x0[...] = first_norm(i_tok[0], z)
 
-    got(S.mod, r.mod_got)
+    got(S.mod, r.mod_got.at[0])
+    push(r.mod_got.at[c], r.mod_got.at[c], S.mod_pair, b, mate)
+    sent(S.mod_pair, r.mod_got.at[0])
+    got(S.mod_pair, r.mod_got.at[0])
     r.mod_flat[...] = jnp.zeros((40, 128), F32)
     for k in range(ALL):
         first = 9 * k // 8
-        r.mod_flat[first : first + 3, :] += r.mod_got[k, 0:3, :]
+        r.mod_flat[first : first + 3, :] += r.mod_got[k % 2, k // 2, 0:3, :]
     for k in range(6):
         row = jnp.concatenate(
             [r.mod_flat[6 * k + t : 6 * k + t + 1, :] for t in range(6)], axis=1

time: 126 us -> 126 us (level)
  no operation moved by 1% of the time
where the time goes in v2:
time: 126 us; the launch traced here: 125 us
  Pallas kernels  123 us (98%)
  between operations  2.78 us (2%)
    pallas_call x1, Pallas kernels, run_layer(): pl.pallas_call(layer_kernel, out_shape=[jax.ShapeDtypeStruct(shape, kind)...  118 us
    pallas_call x1, Pallas kernels, run_finish(): pl.pallas_call(finish_kernel, out_shape=[jax.ShapeDtypeStruct(shape, kind...  4.36 us

profile of v2, /device:TPU:0, one launch (start us, length us, event | category | flops | bytes accessed | tf_op | source)
XLA Modules:
  0.0 125.4 jit_solution(18091893250858021809)
XLA Ops:
  2.6 118.2 %shard_map.382 = (bf16[128,768]{1,0:T(8,128)(2,1)}, f32[128,768]{1,0:T(8,128)}, f32[8,128]{1,0:T(8,128)}, f32[24,2304]{1,0:T(8,128)}, f32[24,768]{1,0:T(8,128)},...) custom-call(s32[1]{0:T(128)S(6)} %copy.44.i_time, ...), custom_call_target="tpu_custom_call" | custom-call | tf_op jit(solution)/shard_map/pallas_call | solution.py:1648
  120.8 4.4 %shard_map.383 = (bf16[1,128,768]{2,1,0:T(8,128)(2,1)}, f32[1,128,768]{2,1,0:T(8,128)}, f32[1,1]{1,0:T(1,128)}, f32[9,24]{1,0:T(8,128)}, f32[9,24]{1,0:T(8,128)}...) custom-call(bf16[128,768]{1,0:T(8,128)(2,1)} %get-tuple-element.53.r, ...), custom_call_target="tpu_custom_call" | custom-call | tf_op jit(solution)/shard_map/pallas_call | solution.py:1728
